TPU v7x, 256 devices: a whole 4x4x8 slice. The times are simulated.
256 devices in a mesh: noise: 8 (over x, core), sample: 32 (over y, z).
Axes of the slice: x: 4, y: 4, z: 8, core: 2. Of those that a mesh axis runs over, the one named last changes fastest.
Arguments:
- noise_latents: bfloat16 [16384, 256], P(('noise', 'sample')), may hold values from -18 to 18
- teacher_latent_rows: bfloat16 [32768, 256], P('sample', 'noise'), may hold values from -6 to 6
Outputs:
- noise_row_potential: float32 [16384], P('noise')
- column_potential: float32 [32768], P('sample')
- targets: bfloat16 [16384, 256], P(('noise', 'sample'))
All inputs are finite; a program needn't handle non-finite values.
Results may differ from a plain program's by a relative error of at most 0.0039.
Values may be sent and summed in bfloat16 or wider, within the bound.
A program may use at most 64 MiB of HBM per device.

v0:
```python
import math
import jax
import jax.numpy as jnp
from jax import lax
from jax.sharding import PartitionSpec as P

ITERS = 3
smoothing_strength = 0.1


def source_logsumexp_partial(scores):
    local_peak = jnp.max(scores, axis=1)
    peak = lax.pmax(local_peak, "sample")
    total = lax.psum(jnp.sum(jnp.exp(scores - peak[:, None]), axis=1), "sample")
    return peak + jnp.log(total)


def col_lse(scores):
    local_peak = jnp.max(scores, axis=0)
    peak = lax.pmax(local_peak, "noise")
    total = lax.psum(jnp.sum(jnp.exp(scores - peak[None, :]), axis=0), "noise")
    return peak + jnp.log(total)


def shards(noise_latents, teacher_latent_rows):
    rows_x = lax.all_gather(noise_latents, "sample", axis=0, tiled=True)
    cols_y = lax.all_gather(teacher_latent_rows, "noise", axis=1, tiled=True)
    embed_dimension = rows_x.shape[1]
    multiplier_coefficient = 1.0 / (embed_dimension * smoothing_strength)
    row_count = rows_x.shape[0]
    col_count = cols_y.shape[0]
    total_rows = row_count * lax.axis_size("noise")
    overall_destination_number = col_count * lax.axis_size("sample")
    xn = jnp.sum(rows_x.astype(jnp.float32) ** 2, axis=1)
    yn = jnp.sum(cols_y.astype(jnp.float32) ** 2, axis=1)

    def kernel():
        inner = jnp.dot(rows_x, cols_y.T, preferred_element_type=jnp.float32)
        return (xn[:, None] + yn[None, :] - 2.0 * inner) * multiplier_coefficient

    def cost():
        return kernel()

    column_potential = jnp.zeros((col_count,), jnp.float32)
    noise_row_potential = jnp.zeros((row_count,), jnp.float32)
    for step in range(ITERS):
        noise_row_potential = -math.log(total_rows) - source_logsumexp_partial(
            column_potential[None, :] - cost()
        )
        column_potential = -math.log(overall_destination_number) - col_lse(
            noise_row_potential[:, None] - cost()
        )
    plan = jnp.exp(noise_row_potential[:, None] + column_potential[None, :] - cost())
    mass_part = jnp.sum(plan, axis=1)
    numer = jnp.dot(plan.astype(jnp.bfloat16), cols_y, preferred_element_type=jnp.float32)
    numer_all, mass_all = lax.psum((numer, mass_part), "sample")
    share = row_count // lax.axis_size("sample")
    start = lax.axis_index("sample") * share
    numer_own = lax.dynamic_slice_in_dim(numer_all, start, share, 0)
    mass_own = lax.dynamic_slice_in_dim(mass_all, start, share, 0)
    targets = (numer_own / mass_own[:, None]).astype(jnp.bfloat16)
    return (noise_row_potential, column_potential, targets)


def solution(mesh):
    placed = (P(("noise", "sample"), None), P("sample", "noise"))
    return jax.shard_map(
        shards,
        mesh=mesh,
        in_specs=placed,
        out_specs=(P("noise"), P("sample"), P(("noise", "sample"), None)),
        check_vma=False,
    )
```

profile of v0, /device:TPU:2, one launch (start us, length us, event | category | flops | bytes accessed | tf_op | source)
XLA Modules:
  0.0 811.2 jit_solution(9159708319463455959)
XLA Ops:
  7.9 13.4 %all_gather.7 = bf16[1024,256]{0,1:T(8,128)(2,1)S(1)} all-gather(bf16[1024,32]{0,1:T(8,128)(2,1)} %param.3), channel_id=1, replica_groups=mesh['noise'=8,'sample'=32] {'noise'}, dimensions={1}, use_global_device_ids=true | all-gather | bytes 589824 | tf_op jit(solution)/shard_map/all_gather | solution.py:27
  21.4 68.3 %all-gather.2.cloned.1.call-done = bf16[2048,256]{1,0:T(8,128)(2,1)} async-done(((bf16[64,256]{1,0:T(8,128)(2,1)}), bf16[2048,256]{1,0:T(8,128)(2,1)}) %all-gather.2.cloned.1.call-update) | async-done | bytes 1048592 | tf_op jit(solution)/shard_map/all_gather | solution.py:26
  91.3 5.6 subtract_reduce_fusion.5
  96.9 73.3 %pmax.42 = f32[2048]{0:T(1024)S(1)} all-reduce(f32[2048]{0:T(1024)S(1)} %get-tuple-element.3), channel_id=1, replica_groups=mesh['noise'=8,'sample'=32] {'sample'}, use_global_device_ids=true, to_apply=%region_3.0 | all-reduce | flops 2048 | bytes 16384 | tf_op jit(solution)/shard_map/pmax | solution.py:13
  170.1 4.8 exponential_reduce_fusion.5
  174.9 70.7 %psum.56 = f32[2048]{0:T(1024)S(1)} all-reduce(f32[2048]{0:T(1024)S(1)} %exponential_reduce_fusion.5), channel_id=1, replica_groups=mesh['noise'=8,'sample'=32] {'sample'}, use_global_device_ids=true, to_apply=%region_5.0 | all-reduce | flops 2048 | bytes 16384 | tf_op jit(solution)/shard_map/psum | solution.py:14
  249.7 10.0 %pmax.43 = f32[1024]{0:T(1024)S(1)} all-reduce(f32[1024]{0:T(1024)S(1)} %subtract_reduce_fusion.4), channel_id=1, replica_groups=mesh['noise'=8,'sample'=32] {'noise'}, use_global_device_ids=true, to_apply=%region_7.0 | all-reduce | flops 1024 | bytes 8192 | tf_op jit(solution)/shard_map/pmax | solution.py:20
  259.7 4.4 exponential_reduce_fusion.4
  264.1 12.4 %psum.57 = f32[1024]{0:T(1024)S(1)} all-reduce(f32[1024]{0:T(1024)S(1)} %exponential_reduce_fusion.4), channel_id=1, replica_groups=mesh['noise'=8,'sample'=32] {'noise'}, use_global_device_ids=true, to_apply=%region_9.0 | all-reduce | flops 1024 | bytes 8192 | tf_op jit(solution)/shard_map/psum | solution.py:21
  280.6 72.6 %pmax.44 = f32[2048]{0:T(1024)S(1)} all-reduce(f32[2048]{0:T(1024)S(1)} %subtract_reduce_fusion.3), channel_id=1, replica_groups=mesh['noise'=8,'sample'=32] {'sample'}, use_global_device_ids=true, to_apply=%region_11.0 | all-reduce | flops 2048 | bytes 16384 | tf_op jit(solution)/shard_map/pmax | solution.py:13
  353.2 4.3 exponential_reduce_fusion.3
  357.5 70.7 %psum.58 = f32[2048]{0:T(1024)S(1)} all-reduce(f32[2048]{0:T(1024)S(1)} %exponential_reduce_fusion.3), channel_id=1, replica_groups=mesh['noise'=8,'sample'=32] {'sample'}, use_global_device_ids=true, to_apply=%region_13.0 | all-reduce | flops 2048 | bytes 16384 | tf_op jit(solution)/shard_map/psum | solution.py:14
  432.2 11.9 %pmax.45 = f32[1024]{0:T(1024)S(1)} all-reduce(f32[1024]{0:T(1024)S(1)} %subtract_reduce_fusion.2), channel_id=1, replica_groups=mesh['noise'=8,'sample'=32] {'noise'}, use_global_device_ids=true, to_apply=%region_15.0 | all-reduce | flops 1024 | bytes 8192 | tf_op jit(solution)/shard_map/pmax | solution.py:20
  444.1 4.4 exponential_reduce_fusion.2
  448.5 12.9 %psum.59 = f32[1024]{0:T(1024)S(1)} all-reduce(f32[1024]{0:T(1024)S(1)} %exponential_reduce_fusion.2), channel_id=1, replica_groups=mesh['noise'=8,'sample'=32] {'noise'}, use_global_device_ids=true, to_apply=%region_17.0 | all-reduce | flops 1024 | bytes 8192 | tf_op jit(solution)/shard_map/psum | solution.py:21
  465.4 72.6 %pmax.46 = f32[2048]{0:T(1024)S(1)} all-reduce(f32[2048]{0:T(1024)S(1)} %subtract_reduce_fusion.1), channel_id=1, replica_groups=mesh['noise'=8,'sample'=32] {'sample'}, use_global_device_ids=true, to_apply=%region_19.0 | all-reduce | flops 2048 | bytes 16384 | tf_op jit(solution)/shard_map/pmax | solution.py:13
  538.0 4.3 exponential_reduce_fusion.1
  542.4 70.9 %psum.60 = f32[2048]{0:T(1024)S(1)} all-reduce(f32[2048]{0:T(1024)S(1)} %exponential_reduce_fusion.1), channel_id=1, replica_groups=mesh['noise'=8,'sample'=32] {'sample'}, use_global_device_ids=true, to_apply=%region_21.0 | all-reduce | flops 2048 | bytes 16384 | tf_op jit(solution)/shard_map/psum | solution.py:14
  617.3 11.9 %pmax.47 = f32[1024]{0:T(1024)S(1)} all-reduce(f32[1024]{0:T(1024)S(1)} %subtract_reduce_fusion), channel_id=1, replica_groups=mesh['noise'=8,'sample'=32] {'noise'}, use_global_device_ids=true, to_apply=%region_23.0 | all-reduce | flops 1024 | bytes 8192 | tf_op jit(solution)/shard_map/pmax | solution.py:20
  629.2 4.4 exponential_reduce_fusion
  633.6 12.9 %psum.61 = f32[1024]{0:T(1024)S(1)} all-reduce(f32[1024]{0:T(1024)S(1)} %exponential_reduce_fusion), channel_id=1, replica_groups=mesh['noise'=8,'sample'=32] {'noise'}, use_global_device_ids=true, to_apply=%region_25.0 | all-reduce | flops 1024 | bytes 8192 | tf_op jit(solution)/shard_map/psum | solution.py:21
  646.5 6.5 fusion.2
  657.3 72.8 %psum.63 = f32[2048]{0:T(1024)S(1)} all-reduce(f32[2048]{0:T(1024)S(1)} %fusion), channel_id=1, replica_groups=mesh['noise'=8,'sample'=32] {'sample'}, use_global_device_ids=true, to_apply=%region_28.0 | all-reduce | flops 2048 | bytes 16384 | tf_op jit(solution)/shard_map/psum | solution.py:56
  730.3 72.6 %all-reduce.2.cloned.1.call-done = f32[2048,256]{1,0:T(8,128)} async-done(((f32[2048,256]{1,0:T(8,128)}), f32[2048,256]{1,0:T(8,128)}) %all-reduce.2.cloned.1.call-update) | async-done | bytes 2097168 | tf_op jit(solution)/shard_map/psum | solution.py:56
  (24 shorter events, 28.5 us)
Async XLA Ops:
  7.2 82.6 %all-gather.2.cloned.1.call-start = ((), (), s32[]{:S(2)}) async-start(), calls=%async_computation | async-start | bytes 1081344 | tf_op jit(solution)/shard_map/all_gather | solution.py:26
  7.9 795.0 %all-reduce.2.cloned.1.call-start = ((), (), s32[]{:S(2)}) async-start(), calls=%async_computation.1 | async-start | bytes 4194304 | tf_op jit(solution)/shard_map/psum | solution.py:56
  613.3 39.7 %copy-start = (f32[2048]{0:T(1024)}, f32[2048]{0:T(1024)S(1)}, u32[]{:S(2)}) copy-start(f32[2048]{0:T(1024)S(1)} %add_subtract_fusion) | copy-start | bytes 24580
  646.5 6.5 copy-start.1
Sparse Core Ops, SparseCore 0:
  10.6 79.1 all-gather.1
  653.1 149.6 all-reduce.1
where the time goes:
time: 812 us; the launch traced here: 811 us
  blocking collectives  589 us (73%)
  waiting for transfers between devices  142 us (17%)
  other arithmetic  54.1 us (7%)
  between operations  14.2 us (2%)
  matrix products  12 us (1%)
    pmax x3, blocking collectives, source_logsumexp_partial(): peak = lax.pmax(local_peak, 'sample')  218 us
    psum x3, blocking collectives, source_logsumexp_partial(): total = lax.psum(jnp.sum(jnp.exp(scores - peak[:, None]), axis=1), 'sample')  212 us
    psum x1, blocking collectives, shards(): numer_all, mass_all = lax.psum((numer, mass_part), 'sample')  72.8 us
    psum x1, waiting for transfers between devices, shards(): numer_all, mass_all = lax.psum((numer, mass_part), 'sample')  72.6 us
    all_gather x1, waiting for transfers between devices, shards(): rows_x = lax.all_gather(noise_latents, 'sample', axis=0, tiled=True)  68.3 us
    psum x3, blocking collectives, col_lse(): total = lax.psum(jnp.sum(jnp.exp(scores - peak[None, :]), axis=0), 'noise')  38.3 us
    pmax x3, blocking collectives, col_lse(): peak = lax.pmax(local_peak, 'noise')  33.8 us
  transfers between devices with their start and end apart: 2, of which 2 were waited for; matrix products, arithmetic and copies ran while one was open for 1% of the time, Pallas kernels for 0%

commit v1 on v0

--- a/solution.py
+++ b/solution.py
@@ -23,7 +23,9 @@
 
 
 def shards(noise_latents, teacher_latent_rows):
-    rows_x = lax.all_gather(noise_latents, "sample", axis=0, tiled=True)
+    rows_x = jnp.concatenate(
+        lax.all_to_all(jnp.stack([noise_latents] * lax.axis_size("sample")), "sample", 0, 0), axis=0
+    )
     cols_y = lax.all_gather(teacher_latent_rows, "noise", axis=1, tiled=True)
     embed_dimension = rows_x.shape[1]
     multiplier_coefficient = 1.0 / (embed_dimension * smoothing_strength)

time: 812 us -> 769 us (0.947)
  waiting for transfers between devices: 142 us -> 87.9 us
  starting transfers between devices: 0.08 us -> 11.5 us
    all_gather x1 -> x0, waiting for transfers between devices: 68.3 us -> none  [shards(): rows_x = lax.all_gather(noise_latents, 'sample', axis=0, tiled=True)]
    all_to_all x0 -> x1, waiting for transfers between devices: none -> 15.1 us  [shards(): lax.all_to_all(jnp.stack([noise_latents] * lax.axis_size('sample')), 'sam...]
    all_to_all x0 -> x1, starting transfers between devices: none -> 11.5 us  [shards(): lax.all_to_all(jnp.stack([noise_latents] * lax.axis_size('sample')), 'sam...]
where the time goes in v1:
time: 769 us; the launch traced here: 768 us
  blocking collectives  589 us (77%)
  waiting for transfers between devices  87.9 us (11%)
  other arithmetic  52.9 us (7%)
  between operations  14.2 us (2%)
  starting transfers between devices  11.5 us (1%)
  matrix products  10.8 us (1%)
    pmax x3, blocking collectives, source_logsumexp_partial(): peak = lax.pmax(local_peak, 'sample')  219 us
    psum x3, blocking collectives, source_logsumexp_partial(): total = lax.psum(jnp.sum(jnp.exp(scores - peak[:, None]), axis=1), 'sample')  212 us
    psum x1, blocking collectives, shards(): numer_all, mass_all = lax.psum((numer, mass_part), 'sample')  72.9 us
    psum x1, waiting for transfers between devices, shards(): numer_all, mass_all = lax.psum((numer, mass_part), 'sample')  72.8 us
    psum x3, blocking collectives, col_lse(): total = lax.psum(jnp.sum(jnp.exp(scores - peak[None, :]), axis=0), 'noise')  38.3 us
    pmax x3, blocking collectives, col_lse(): peak = lax.pmax(local_peak, 'noise')  33.7 us
  transfers between devices with their start and end apart: 2, of which 2 were waited for; matrix products, arithmetic and copies ran while one was open for 1% of the time, Pallas kernels for 0%

profile of v1, /device:TPU:2, one launch (start us, length us, event | category | flops | bytes accessed | tf_op | source)
XLA Modules:
  0.0 768.3 jit_solution(16960596037401111321)
XLA Ops:
  9.0 11.5 %all-to-all-start = ((bf16[32,64,256]{2,1,0:T(8,128)(2,1)}), bf16[32,64,256]{2,1,0:T(8,128)(2,1)S(1)}, u32[]{:S(2)}, u32[]{:S(2)}) async-start(bf16[32,64,256]{2,1,0:T(8,128)(2,1)} %stack.2), calls=%async_computation | async-start | bytes 2097152 | tf_op jit(solution)/shard_map/all_to_all | solution.py:27
  20.6 13.4 %all_gather.3 = bf16[1024,256]{0,1:T(8,128)(2,1)S(1)} all-gather(bf16[1024,32]{0,1:T(8,128)(2,1)} %param.3), channel_id=1, replica_groups=mesh['noise'=8,'sample'=32] {'noise'}, dimensions={1}, use_global_device_ids=true | all-gather | bytes 589824 | tf_op jit(solution)/shard_map/all_gather | solution.py:29
  34.1 15.1 %all-to-all-done = bf16[32,64,256]{2,1,0:T(8,128)(2,1)S(1)} async-done(((bf16[32,64,256]{2,1,0:T(8,128)(2,1)}), bf16[32,64,256]{2,1,0:T(8,128)(2,1)S(1)}, u32[]{:S(2)}, u32[]{:S(2)}) %all-to-all-start) | async-done | bytes 1048608 | tf_op jit(solution)/shard_map/all_to_all | solution.py:27
  49.6 4.3 subtract_reduce_fusion.5
  53.9 73.0 %pmax.42 = f32[2048]{0:T(1024)S(1)} all-reduce(f32[2048]{0:T(1024)S(1)} %get-tuple-element.3), channel_id=1, replica_groups=mesh['noise'=8,'sample'=32] {'sample'}, use_global_device_ids=true, to_apply=%region_3.0 | all-reduce | flops 2048 | bytes 16384 | tf_op jit(solution)/shard_map/pmax | solution.py:13
  126.9 4.8 exponential_reduce_fusion.5
  131.6 70.6 %psum.56 = f32[2048]{0:T(1024)S(1)} all-reduce(f32[2048]{0:T(1024)S(1)} %exponential_reduce_fusion.5), channel_id=1, replica_groups=mesh['noise'=8,'sample'=32] {'sample'}, use_global_device_ids=true, to_apply=%region_5.0 | all-reduce | flops 2048 | bytes 16384 | tf_op jit(solution)/shard_map/psum | solution.py:14
  206.3 10.0 %pmax.43 = f32[1024]{0:T(1024)S(1)} all-reduce(f32[1024]{0:T(1024)S(1)} %subtract_reduce_fusion.4), channel_id=1, replica_groups=mesh['noise'=8,'sample'=32] {'noise'}, use_global_device_ids=true, to_apply=%region_7.0 | all-reduce | flops 1024 | bytes 8192 | tf_op jit(solution)/shard_map/pmax | solution.py:20
  216.4 4.4 exponential_reduce_fusion.4
  220.7 12.4 %psum.57 = f32[1024]{0:T(1024)S(1)} all-reduce(f32[1024]{0:T(1024)S(1)} %exponential_reduce_fusion.4), channel_id=1, replica_groups=mesh['noise'=8,'sample'=32] {'noise'}, use_global_device_ids=true, to_apply=%region_9.0 | all-reduce | flops 1024 | bytes 8192 | tf_op jit(solution)/shard_map/psum | solution.py:21
  237.2 72.8 %pmax.44 = f32[2048]{0:T(1024)S(1)} all-reduce(f32[2048]{0:T(1024)S(1)} %subtract_reduce_fusion.3), channel_id=1, replica_groups=mesh['noise'=8,'sample'=32] {'sample'}, use_global_device_ids=true, to_apply=%region_11.0 | all-reduce | flops 2048 | bytes 16384 | tf_op jit(solution)/shard_map/pmax | solution.py:13
  310.0 4.3 exponential_reduce_fusion.3
  314.3 70.6 %psum.58 = f32[2048]{0:T(1024)S(1)} all-reduce(f32[2048]{0:T(1024)S(1)} %exponential_reduce_fusion.3), channel_id=1, replica_groups=mesh['noise'=8,'sample'=32] {'sample'}, use_global_device_ids=true, to_apply=%region_13.0 | all-reduce | flops 2048 | bytes 16384 | tf_op jit(solution)/shard_map/psum | solution.py:14
  389.0 11.9 %pmax.45 = f32[1024]{0:T(1024)S(1)} all-reduce(f32[1024]{0:T(1024)S(1)} %subtract_reduce_fusion.2), channel_id=1, replica_groups=mesh['noise'=8,'sample'=32] {'noise'}, use_global_device_ids=true, to_apply=%region_15.0 | all-reduce | flops 1024 | bytes 8192 | tf_op jit(solution)/shard_map/pmax | solution.py:20
  400.8 4.4 exponential_reduce_fusion.2
  405.2 12.9 %psum.59 = f32[1024]{0:T(1024)S(1)} all-reduce(f32[1024]{0:T(1024)S(1)} %exponential_reduce_fusion.2), channel_id=1, replica_groups=mesh['noise'=8,'sample'=32] {'noise'}, use_global_device_ids=true, to_apply=%region_17.0 | all-reduce | flops 1024 | bytes 8192 | tf_op jit(solution)/shard_map/psum | solution.py:21
  422.1 72.8 %pmax.46 = f32[2048]{0:T(1024)S(1)} all-reduce(f32[2048]{0:T(1024)S(1)} %subtract_reduce_fusion.1), channel_id=1, replica_groups=mesh['noise'=8,'sample'=32] {'sample'}, use_global_device_ids=true, to_apply=%region_19.0 | all-reduce | flops 2048 | bytes 16384 | tf_op jit(solution)/shard_map/pmax | solution.py:13
  499.3 70.8 %psum.60 = f32[2048]{0:T(1024)S(1)} all-reduce(f32[2048]{0:T(1024)S(1)} %exponential_reduce_fusion.1), channel_id=1, replica_groups=mesh['noise'=8,'sample'=32] {'sample'}, use_global_device_ids=true, to_apply=%region_21.0 | all-reduce | flops 2048 | bytes 16384 | tf_op jit(solution)/shard_map/psum | solution.py:14
  574.1 11.9 %pmax.47 = f32[1024]{0:T(1024)S(1)} all-reduce(f32[1024]{0:T(1024)S(1)} %subtract_reduce_fusion), channel_id=1, replica_groups=mesh['noise'=8,'sample'=32] {'noise'}, use_global_device_ids=true, to_apply=%region_23.0 | all-reduce | flops 1024 | bytes 8192 | tf_op jit(solution)/shard_map/pmax | solution.py:20
  586.0 4.4 exponential_reduce_fusion
  590.3 12.9 %psum.61 = f32[1024]{0:T(1024)S(1)} all-reduce(f32[1024]{0:T(1024)S(1)} %exponential_reduce_fusion), channel_id=1, replica_groups=mesh['noise'=8,'sample'=32] {'noise'}, use_global_device_ids=true, to_apply=%region_25.0 | all-reduce | flops 1024 | bytes 8192 | tf_op jit(solution)/shard_map/psum | solution.py:21
  603.3 6.5 fusion.2
  614.1 72.9 %psum.63 = f32[2048]{0:T(1024)S(1)} all-reduce(f32[2048]{0:T(1024)S(1)} %fusion), channel_id=1, replica_groups=mesh['noise'=8,'sample'=32] {'sample'}, use_global_device_ids=true, to_apply=%region_28.0 | all-reduce | flops 2048 | bytes 16384 | tf_op jit(solution)/shard_map/psum | solution.py:58
  687.1 72.8 %all-reduce.2.cloned.1.call-done = f32[2048,256]{1,0:T(8,128)} async-done(((f32[2048,256]{1,0:T(8,128)}), f32[2048,256]{1,0:T(8,128)}) %all-reduce.2.cloned.1.call-update) | async-done | bytes 2097168 | tf_op jit(solution)/shard_map/psum | solution.py:58
  (25 shorter events, 32.8 us)
Async XLA Ops:
  9.0 40.1 %all-to-all-start = ((bf16[32,64,256]{2,1,0:T(8,128)(2,1)}), bf16[32,64,256]{2,1,0:T(8,128)(2,1)S(1)}, u32[]{:S(2)}, u32[]{:S(2)}) async-start(bf16[32,64,256]{2,1,0:T(8,128)(2,1)} %stack.2), calls=%async_computation | async-start | bytes 2097152 | tf_op jit(solution)/shard_map/all_to_all | solution.py:27
  20.5 739.4 %all-reduce.2.cloned.1.call-start = ((), (), s32[]{:S(2)}) async-start(), calls=%async_computation.1 | async-start | bytes 4194304 | tf_op jit(solution)/shard_map/psum | solution.py:58
  570.1 39.7 %copy-start = (f32[2048]{0:T(1024)}, f32[2048]{0:T(1024)S(1)}, u32[]{:S(2)}) copy-start(f32[2048]{0:T(1024)S(1)} %add_subtract_fusion) | copy-start | bytes 24580
  603.3 6.5 copy-start.1
Sparse Core Ops, SparseCore 0:
  609.9 149.9 all-reduce.1
